TPU v7x, 32 devices: a whole 2x2x4 slice. The times are simulated.
32 devices in a mesh: group: 2 (over y), patch: 4 (over z), head: 2 (over x), cfg: 2 (over core).
Axes of the slice: x: 2, y: 2, z: 4, core: 2. Of those that a mesh axis runs over, the one named last changes fastest.
Arguments:
- fresh_query: bfloat16 [4, 256, 2560], P(('group', 'cfg'), ('patch', 'head')), parts along dimension 0, may hold values from -32 to 32
- fresh_key: bfloat16 [4, 256, 2560], P(('group', 'cfg'), ('patch', 'head')), parts along dimension 0, may hold values from -9 to 9
- fresh_value: bfloat16 [4, 256, 2560], P(('group', 'cfg'), ('patch', 'head')), parts along dimension 0, may hold values from -12 to 12
- stale_key: bfloat16 [4, 256, 2560], P(('group', 'cfg'), 'patch', 'head'), parts along dimension 0, may hold values from -8 to 8
- stale_value: bfloat16 [4, 256, 2560], P(('group', 'cfg'), 'patch', 'head'), parts along dimension 0, may hold values from -12 to 12
- cross_query: bfloat16 [4, 256, 2560], P(('group', 'cfg'), ('patch', 'head')), parts along dimension 0, may hold values from -32 to 32
- text_key: bfloat16 [4, 512, 2560], P(('group', 'cfg'), None, 'head'), parts along dimension 0, may hold values from -8 to 8
- text_value: bfloat16 [4, 512, 2560], P(('group', 'cfg'), None, 'head'), parts along dimension 0, may hold values from -12 to 12
- text_mask: int32 [4, 512], P(('group', 'cfg')), parts along dimension 0, may hold values from 0 to 1, as said below
Outputs:
- self_mixed: bfloat16 [4, 256, 2560], P(('group', 'cfg'), ('patch', 'head')), parts along dimension 0
- cross_mixed: bfloat16 [4, 256, 2560], P(('group', 'cfg'), ('patch', 'head')), parts along dimension 0
There are 2 independent parts, one for each index of `group`. A program takes and returns all parts, laid end to end along the dimension named above; each array names one. Nothing has to cross between parts.
Inputs may be any that keep to these rules, and one draw needn't show every extreme that they name: In each branch the ones of text_mask form a prefix of 32 or more positions; in one of the two branches all 512 are ones, in the other some are zeros.
All inputs are finite; a program needn't handle non-finite values.
Results may differ from a plain program's by a relative error of at most 0.005.
Values may be sent and summed in bfloat16 or wider, within the bound.
No kernel may reach another device: no remote copies, remote signals or barrier semaphores. Data moves between devices by JAX's collectives and lax.ppermute only.
A program may use at most 128 MiB of HBM per device.

v0:
```python
import math

import jax
import jax.numpy as jnp
from jax import lax
from jax.experimental import pallas as pl
from jax.experimental.pallas import tpu as pltpu
from jax.sharding import PartitionSpec as P

HD = 128
SCALE = 1.0 / math.sqrt(HD)


def scores_of(queries, keys):
    return lax.dot_general(
        queries, keys, (((1,), (1,)), ((), ())), preferred_element_type=jnp.float32
    ) * SCALE


def weighted(weights, values):
    return lax.dot_general(
        weights, values, (((1,), (0,)), ((), ())), preferred_element_type=jnp.float32
    )


def softmax_parts(scores):
    weights = jnp.exp(scores - jnp.max(scores, axis=-1, keepdims=True))
    totals = jnp.sum(weights, axis=-1, keepdims=True)
    shares = jnp.broadcast_to(1.0 / totals, (scores.shape[0], HD))
    return weights.astype(jnp.bfloat16), shares


def run_all(copies, sems):
    started = []
    for index, (source, target) in enumerate(copies):
        started.append(pltpu.make_async_copy(source, target, sems.at[index]))
        started[-1].start()
    for copy in started:
        copy.wait()


def load_kernel(*refs):
    half = len(refs) // 2
    run_all(zip(refs[:half], refs[half:-1]), refs[-1])


def gate_kernel(*refs):
    pass


def head_lanes(head):
    return slice(head * HD, (head + 1) * HD)


def cross_kernel(shards, *refs):
    queries, (key_ref, value_ref, mask_ref) = refs[:shards], refs[shards : shards + 3]
    targets, (weights_ref, shares_ref) = refs[2 * shards + 2 : -2], refs[-2:]
    rows, cols = targets[0].shape
    usable = mask_ref[...] > 0
    for head in range(cols // HD):
        lanes = head_lanes(head)
        scores = scores_of(
            jnp.concatenate([ref[:, lanes] for ref in queries], axis=0), key_ref[0, :, lanes]
        )
        weights_ref[head], shares_ref[head] = softmax_parts(jnp.where(usable, scores, -jnp.inf))
    for head in range(cols // HD):
        lanes = head_lanes(head)
        mixed = weighted(weights_ref[head], value_ref[0, :, lanes]) * shares_ref[head]
        for place, target in enumerate(targets):
            target[:, lanes] = mixed[place * rows : (place + 1) * rows].astype(target.dtype)


def solution(mesh):
    shards = mesh.shape["head"]
    patches = mesh.shape["patch"]
    axes = ("patch", "head")
    vmem = pl.BlockSpec(memory_space=pltpu.VMEM)
    hbm = pl.BlockSpec(memory_space=pltpu.HBM)
    anywhere = pl.BlockSpec(memory_space=pl.ANY)
    params = pltpu.CompilerParams(vmem_limit_bytes=32 * 1024 * 1024)

    def call(kernel, name, out_shape, operands, out_spec=vmem, in_spec=vmem, scratch=(), **more):
        return pl.pallas_call(
            kernel,
            out_shape=out_shape,
            in_specs=[in_spec] * len(operands),
            out_specs=jax.tree.map(lambda _: out_spec, out_shape),
            scratch_shapes=scratch,
            compiler_params=params,
            name=name,
            **more,
        )(*operands)

    def in_hbm(*arrays):
        return [pltpu.with_memory_space_constraint(a, pltpu.HBM) for a in arrays]

    def handed_on(arrays):
        return call(
            gate_kernel,
            "gate",
            [jax.ShapeDtypeStruct(a.shape, a.dtype) for a in arrays],
            arrays,
            anywhere,
            anywhere,
            input_output_aliases={i: i for i in range(len(arrays))},
            cost_estimate=pl.CostEstimate(flops=500000000, bytes_accessed=1800000, transcendentals=0),
        )

    def per_device(
        fresh_query,
        fresh_key,
        fresh_value,
        stale_key,
        stale_value,
        cross_query,
        text_key,
        text_value,
        text_mask,
    ):
        rows, full = fresh_query.shape[1:]
        patch_rows = stale_key.shape[1]
        text_rows = text_key.shape[1]
        kind = fresh_query.dtype
        cols = full // shards
        heads = cols // HD
        share = math.gcd(patches, heads)
        teams = patches // share
        width = cols // share
        share_heads = heads // share
        mates = [(j, s) for j in range(share) for s in range(shards) if (j, s) != (0, 0)]

        ring = list(range(0, teams, 2)) + list(range(1, teams, 2))[::-1]
        ring_next = dict(zip(ring, ring[1:] + ring[:1]))

        def moved(array, step, shift, turn):
            pairs = []
            for patch in range(patches):
                team, member = divmod(patch, share)
                team = ring_next[team] if step else team
                target = team * share + (member + shift) % share
                for shard in range(shards):
                    pairs.append(
                        (patch * shards + shard, target * shards + (shard + turn) % shards)
                    )
            return lax.ppermute(array, axes, pairs)

        def place_of(shift, turn, ref, size):
            shard = lax.rem(lax.axis_index("head") + turn, shards)
            member = lax.rem(lax.axis_index("patch") + shift, share)
            start = pl.multiple_of(shard * cols + member * width, HD)
            return ref.at[0, :, pl.ds(start, size)]

        stale_rows = 2 * patch_rows

        def fresh_start(shift, turn):
            return stale_rows if turn == 0 and shift != 0 else 0

        def message_rows(shift, turn):
            return fresh_start(shift, turn) + 3 * rows

        def pack_kernel(query, key, value, old_key, old_value, cross, *refs):
            stale, own, refs = refs[:share], refs[share], refs[share + 1 :]
            crosses, messages = refs[:shards], refs[shards:-1]
            me = lax.rem(lax.axis_index("patch"), share)
            copies = []

            def stale_copies(shift, target):
                part = lax.rem(me + shift, share)
                lanes = pl.ds(pl.multiple_of(part * width, HD), width)
                for index, source in enumerate((old_key, old_value)):
                    block = pl.ds(index * patch_rows, patch_rows)
                    copies.append((source.at[0, :, lanes], target.at[block]))

            def fresh_copies(shift, turn, target, first):
                for index, source in enumerate((query, key, value)):
                    block = pl.ds(first + index * rows, rows)
                    copies.append((place_of(shift, turn, source, width), target.at[block]))

            for (shift, turn), message in zip(mates, messages):
                first = fresh_start(shift, turn)
                if first:
                    stale_copies(shift, message)
                fresh_copies(shift, turn, message, first)
            for shift in range(share):
                stale_copies(shift, stale[shift])
            fresh_copies(0, 0, own, 0)
            for turn, target in enumerate(crosses):
                shard = lax.rem(lax.axis_index("head") + turn, shards)
                lanes = pl.ds(pl.multiple_of(shard * cols, HD), cols)
                copies.append((cross.at[0, :, lanes], target))
            run_all(copies, refs[-1])

        packed_shapes = (
            [(stale_rows, width)] * share
            + [(3 * rows, width)]
            + [(rows, cols)] * shards
            + [(message_rows(*mate), width) for mate in mates]
        )
        copy_count = 2 * share + 3 + shards + sum(
            3 + (2 if fresh_start(*mate) else 0) for mate in mates
        )
        packed = call(
            pack_kernel,
            "pack",
            [pltpu.VMEM(shape, kind) for shape in packed_shapes],
            in_hbm(fresh_query, fresh_key, fresh_value, stale_key, stale_value, cross_query),
            in_spec=hbm,
            scratch=[pltpu.SemaphoreType.DMA((copy_count,))],
        )
        stale, own, packed = packed[:share], packed[share], packed[share + 1 :]
        crosses, messages = packed[:shards], packed[shards:]
        arrived = [
            moved(message, 0, *mate) for mate, message in zip(mates, messages)
        ]
        crosses = [crosses[0]] + [moved(a, 0, 0, turn) for turn, a in enumerate(crosses) if turn]

        pieces = []
        if teams > 1:
            latest = [moved(stale[shift], 1, shift, 0) for shift in range(share)]
            pieces += latest
            for _ in range(teams - 2):
                latest = [moved(piece, 1, 0, 0) for piece in latest]
                pieces += latest

        pieces = handed_on(pieces) if pieces else pieces

        text = [text_key, text_value, text_mask]
        text = call(
            load_kernel,
            "load",
            [pltpu.VMEM(a.shape, a.dtype) for a in text],
            in_hbm(*text),
            in_spec=hbm,
            scratch=[pltpu.SemaphoreType.DMA((len(text),))],
        )

        from_shards = [a for (shift, _), a in zip(mates, arrived) if shift == 0]
        cross_own, *cross_away = call(
            lambda *refs: cross_kernel(shards, *refs),
            "cross",
            [pltpu.VMEM((rows, cols), kind)] * shards,
            (*crosses, *text, *from_shards),
            scratch=[
                pltpu.VMEM((heads, shards * rows, text_rows), kind),
                pltpu.VMEM((heads, shards * rows, HD), jnp.float32),
            ],
        )
        cross_back = [moved(a, 0, 0, -turn - 1) for turn, a in enumerate(cross_away)]

        def place_kernel(spots, size, *refs):
            run_all(
                [
                    (ref, place_of(shift, turn, refs[-2], size))
                    for (shift, turn), ref in zip(spots, refs[:-2])
                ],
                refs[-1],
            )

        def cross_place_kernel(*refs):
            copies = []
            for turn, ref in enumerate(refs[:-2]):
                shard = lax.rem(lax.axis_index("head") + turn, shards)
                start = pl.multiple_of(shard * cols, HD)
                copies.append((ref, refs[-2].at[0, :, pl.ds(start, cols)]))
            run_all(copies, refs[-1])

        whole = jax.ShapeDtypeStruct((1, rows, full), kind)
        cross_mixed = call(
            cross_place_kernel,
            "place_cross",
            whole,
            (cross_own, *cross_back),
            hbm,
            scratch=[pltpu.SemaphoreType.DMA((shards,))],
        )

        spots = [(0, 0)] + mates
        tokens = [own, *arrived]
        first_row = dict(zip(spots, [0] + [fresh_start(*mate) for mate in mates]))

        def token_rows(refs, shift, index, lanes):
            found = []
            for spot, ref in zip(spots, refs):
                if spot[0] == shift:
                    start = first_row[spot] + index * rows
                    found.append(ref[start : start + rows, lanes])
            return found

        def stale_of(refs, shift, index, lanes):
            own_stale, *others = refs[len(spots) :]
            found = []
            if shift != 0:
                found.append(own_stale)
            found += [
                ref for (other, turn), ref in zip(spots, refs) if turn == 0 and other not in (0, shift)
            ]
            block = slice(index * patch_rows, (index + 1) * patch_rows)
            return [ref[block, lanes] for ref in found + others]

        def weights_kernel(*refs):
            sources, targets = refs[: -2 * len(spots)], refs[-2 * len(spots) :]
            for head in range(share_heads):
                lanes = head_lanes(head)
                for shift in range(share):
                    queries = token_rows(sources, shift, 0, lanes)
                    keys = token_rows(sources, shift, 1, lanes) + stale_of(sources, shift, 0, lanes)
                    weights, shares = softmax_parts(
                        scores_of(jnp.concatenate(queries, axis=0), jnp.concatenate(keys, axis=0))
                    )
                    for turn in range(shards):
                        spot = spots.index((shift, turn))
                        block = slice(turn * rows, (turn + 1) * rows)
                        targets[2 * spot][head] = weights[block]
                        targets[2 * spot + 1][head] = shares[block]

        def mix_kernel(shift, weights_ref, shares_ref, *refs):
            sources, target = refs[:-1], refs[-1]
            for head in range(share_heads):
                lanes = head_lanes(head)
                values = token_rows(sources, shift, 2, lanes) + stale_of(sources, shift, 1, lanes)
                mixed = weighted(weights_ref[head], jnp.concatenate(values, axis=0))
                target[:, lanes] = (mixed * shares_ref[head]).astype(target.dtype)

        sources = (*tokens, stale[0], *pieces)
        parts = call(
            weights_kernel,
            "weights",
            [
                pltpu.VMEM((share_heads, rows, patch_rows * patches), kind),
                pltpu.VMEM((share_heads, rows, HD), jnp.float32),
            ]
            * len(spots),
            sources,
        )

        def mixed(spot):
            return call(
                lambda *refs: mix_kernel(spots[spot][0], *refs),
                "mix",
                pltpu.VMEM((rows, width), kind),
                (*parts[2 * spot : 2 * spot + 2], *sources),
            )

        back = [
            moved(mixed(index), 0, -shift, -turn)
            for index, (shift, turn) in enumerate(spots)
            if index > 0
        ]
        self_mixed = call(
            lambda *refs: place_kernel(spots, width, *refs),
            "place_self",
            whole,
            (mixed(0), *back),
            hbm,
            scratch=[pltpu.SemaphoreType.DMA((len(spots),))],
        )
        return (self_mixed, cross_mixed)

    token = P(("group", "cfg"), ("patch", "head"), None)
    stale = P(("group", "cfg"), "patch", "head")
    text = P(("group", "cfg"), None, "head")
    return jax.shard_map(
        per_device,
        mesh=mesh,
        in_specs=(token, token, token, stale, stale, token, text, text, P(("group", "cfg"), None)),
        out_specs=(token, token),
        check_vma=False,
    )
```

profile of v0, /device:TPU:0, one launch (start us, length us, event | category | flops | bytes accessed | tf_op | source)
XLA Modules:
  0.0 31.2 jit_solution(6185894903795486930)
XLA Ops:
  0.6 1.5 %pack.1 = (bf16[128,640]{1,0:T(8,128)(2,1)S(1)}, bf16[128,640]{1,0:T(8,128)(2,1)S(1)}, bf16[96,640]{1,0:T(8,128)(2,1)S(1)}, bf16[32,1280]{1,0:T(8,128)(2,1)S(1)}...) custom-call(bf16[1,32,2560]{2,1,0:T(8,128)(2,1)} %query.1, ...), custom_call_target="tpu_custom_call" | custom-call | tf_op jit(solution)/shard_map/pack/pallas_call | solution.py:83
  2.2 3.1 %collective-permute-start.1 = (bf16[224,640]{1,0:T(8,128)(2,1)S(1)}, bf16[224,640]{1,0:T(8,128)(2,1)S(1)}, u32[]{:S(2)}, u32[]{:S(2)}) collective-permute-start(bf16[224,640]{1,0:T(8,128)(2,1)S(1)} %get-tuple-element.27), channel_id=1, source_target_pairs={{0,4},{2,6},{4,0},{6,2},{8,12},{10,14},{12,8},{14,10},{1,5},{3,7},... | collective-permute-start | bytes 860168 | tf_op jit(solution)/shard_map/ppermute | solution.py:145
  5.2 2.5 %collective-permute-start.4 = (bf16[128,640]{1,0:T(8,128)(2,1)S(1)}, bf16[128,640]{1,0:T(8,128)(2,1)S(1)}, u32[]{:S(2)}, u32[]{:S(2)}) collective-permute-start(bf16[128,640]{1,0:T(8,128)(2,1)S(1)} %get-tuple-element.30), channel_id=1, source_target_pairs={{0,12},{2,14},{4,8},{6,10},{8,4},{10,6},{12,0},{14,2},{1,13},{3,15... | collective-permute-start | bytes 491528 | tf_op jit(solution)/shard_map/ppermute | solution.py:145
  7.7 0.1 collective-permute-start.3
  7.8 1.5 %collective-permute-start.8 = (bf16[32,1280]{1,0:T(8,128)(2,1)S(1)}, bf16[32,1280]{1,0:T(8,128)(2,1)S(1)}, u32[]{:S(2)}, u32[]{:S(2)}) collective-permute-start(bf16[32,1280]{1,0:T(8,128)(2,1)S(1)} %get-tuple-element.42), channel_id=1, source_target_pairs={{0,2},{2,0},{4,6},{6,4},{8,10},{10,8},{12,14},{14,12},{1,3},{3,1},... | collective-permute-start | bytes 245768 | tf_op jit(solution)/shard_map/ppermute | solution.py:145
  9.3 0.5 %collective-permute-start = (bf16[96,640]{1,0:T(8,128)(2,1)S(1)}, bf16[96,640]{1,0:T(8,128)(2,1)S(1)}, u32[]{:S(2)}, u32[]{:S(2)}) collective-permute-start(bf16[96,640]{1,0:T(8,128)(2,1)S(1)} %get-tuple-element.26), channel_id=1, source_target_pairs={{0,2},{2,0},{4,6},{6,4},{8,10},{10,8},{12,14},{14,12},{1,3},{3,1},... | collective-permute-start | bytes 368648 | tf_op jit(solution)/shard_map/ppermute | solution.py:145
  9.9 3.2 %collective-permute-done.8.refs_1_ = bf16[32,1280]{1,0:T(8,128)(2,1)S(1)} collective-permute-done((bf16[32,1280]{1,0:T(8,128)(2,1)S(1)}, bf16[32,1280]{1,0:T(8,128)(2,1)S(1)}, u32[]{:S(2)}, u32[]{:S(2)}) %collective-permute-start.8) | collective-permute-done | bytes 81952 | tf_op jit(solution)/shard_map/ppermute | solution.py:145
  13.1 2.1 %collective-permute-start.2 = (bf16[96,640]{1,0:T(8,128)(2,1)S(1)}, bf16[96,640]{1,0:T(8,128)(2,1)S(1)}, u32[]{:S(2)}, u32[]{:S(2)}) collective-permute-start(bf16[96,640]{1,0:T(8,128)(2,1)S(1)} %get-tuple-element.28), channel_id=1, source_target_pairs={{0,6},{2,4},{4,2},{6,0},{8,14},{10,12},{12,10},{14,8},{1,7},{3,5},... | collective-permute-start | bytes 368648 | tf_op jit(solution)/shard_map/ppermute | solution.py:145
  15.2 1.7 %load.1 = (bf16[1,512,1280]{2,1,0:T(8,128)(2,1)S(1)}, bf16[1,512,1280]{2,1,0:T(8,128)(2,1)S(1)}, s32[1,512]{1,0:T(1,128)S(1)}) custom-call(bf16[1,512,1280]{2,1,0:T(8,128)(2,1)} %refs_0_.1, bf16[1,512,1280]{2,1,0:T(8,128)(2,1)} %refs_1_.1, s32[1,512]{1,0:T(1,128)} %refs_2_.1), custom_call_target="tpu_custom_call" | custom-call | tf_op jit(solution)/shard_map/load/pallas_call | solution.py:83
  17.0 0.0 collective-permute-done.refs_1_.refs_3_.refs_5_
  17.0 0.9 %cross.3 = (bf16[32,1280]{1,0:T(8,128)(2,1)S(1)}, bf16[32,1280]{1,0:T(8,128)(2,1)S(1)}) custom-call(bf16[32,1280]{1,0:T(8,128)(2,1)S(1)} %get-tuple-element.41.refs_0_, bf16[32,1280]{1,0:T(8,128)(2,1)S(1)} %collective-permute-done.8.refs_1_, bf16[1,512,1280]{2,1,0:T(8,128)(2,1)S(1)} %get-tuple-element.43.refs_2_, ...), custom_call_target="tpu_custom_call" | custom-call | tf_op jit(solution)/shard_map/cross/pallas_call | solution.py:83
  17.8 0.9 %collective-permute-start.9 = (bf16[32,1280]{1,0:T(8,128)(2,1)S(1)}, bf16[32,1280]{1,0:T(8,128)(2,1)S(1)}, u32[]{:S(2)}, u32[]{:S(2)}) collective-permute-start(bf16[32,1280]{1,0:T(8,128)(2,1)S(1)} %get-tuple-element.47), channel_id=1, source_target_pairs={{0,2},{2,0},{4,6},{6,4},{8,10},{10,8},{12,14},{14,12},{1,3},{3,1},... | collective-permute-start | bytes 245768 | tf_op jit(solution)/shard_map/ppermute | solution.py:145
  18.8 0.2 collective-permute-done.4.refs_1_
  18.9 3.3 %collective-permute-done.3.refs_0_ = bf16[128,640]{1,0:T(8,128)(2,1)S(1)} collective-permute-done((bf16[128,640]{1,0:T(8,128)(2,1)S(1)}, bf16[128,640]{1,0:T(8,128)(2,1)S(1)}, u32[]{:S(2)}, u32[]{:S(2)}) %collective-permute-start.3) | collective-permute-done | bytes 163872 | tf_op jit(solution)/shard_map/ppermute | solution.py:145
  22.2 0.3 collective-permute-done.2.refs_3_.refs_5_
  22.5 0.0 collective-permute-done.1.refs_2_.refs_4_
  22.5 0.5 %weights.1 = (bf16[5,32,256]{2,1,0:T(8,128)(2,1)S(1)}, f32[5,32,128]{2,1,0:T(8,128)S(1)}, bf16[5,32,256]{2,1,0:T(8,128)(2,1)S(1)}, f32[5,32,128]{2,1,0:T(8,128)S...) custom-call(bf16[96,640]{1,0:T(8,128)(2,1)S(1)} %get-tuple-element.2, ...), custom_call_target="tpu_custom_call" | custom-call | tf_op jit(solution)/shard_map/weights/pallas_call | solution.py:83
  23.0 0.2 mix.7
  23.2 2.1 %collective-permute-start.7 = (bf16[32,640]{1,0:T(8,128)(2,1)S(1)}, bf16[32,640]{1,0:T(8,128)(2,1)S(1)}, u32[]{:S(2)}, u32[]{:S(2)}) collective-permute-start(bf16[32,640]{1,0:T(8,128)(2,1)S(1)} %mix.7), channel_id=1, source_target_pairs={{0,6},{2,4},{4,2},{6,0},{8,14},{10,12},{12,10},{14,8},{1,7},{3,5},... | collective-permute-start | bytes 122888 | tf_op jit(solution)/shard_map/ppermute | solution.py:145
  25.3 0.2 mix.6
  25.5 0.7 %collective-permute-start.6 = (bf16[32,640]{1,0:T(8,128)(2,1)S(1)}, bf16[32,640]{1,0:T(8,128)(2,1)S(1)}, u32[]{:S(2)}, u32[]{:S(2)}) collective-permute-start(bf16[32,640]{1,0:T(8,128)(2,1)S(1)} %mix.6), channel_id=1, source_target_pairs={{0,4},{2,6},{4,0},{6,2},{8,12},{10,14},{12,8},{14,10},{1,5},{3,7},... | collective-permute-start | bytes 122888 | tf_op jit(solution)/shard_map/ppermute | solution.py:145
  26.2 0.2 mix.5
  26.4 0.9 %collective-permute-start.5 = (bf16[32,640]{1,0:T(8,128)(2,1)S(1)}, bf16[32,640]{1,0:T(8,128)(2,1)S(1)}, u32[]{:S(2)}, u32[]{:S(2)}) collective-permute-start(bf16[32,640]{1,0:T(8,128)(2,1)S(1)} %mix.5), channel_id=1, source_target_pairs={{0,2},{2,0},{4,6},{6,4},{8,10},{10,8},{12,14},{14,12},{1,3},{3,1},... | collective-permute-start | bytes 122888 | tf_op jit(solution)/shard_map/ppermute | solution.py:145
  27.3 0.0 collective-permute-done.9.refs_1_
  27.3 0.7 %place_cross.1 = bf16[1,32,2560]{2,1,0:T(8,128)(2,1)} custom-call(bf16[32,1280]{1,0:T(8,128)(2,1)S(1)} %get-tuple-element.46.refs_0_, bf16[32,1280]{1,0:T(8,128)(2,1)S(1)} %collective-permute-done.9.refs_1_), custom_call_target="tpu_custom_call" | custom-call | tf_op jit(solution)/shard_map/place_cross/pallas_call | solution.py:83
  28.0 0.2 mix.4.refs_0_
  28.2 0.3 %collective-permute-done.7.refs_3_ = bf16[32,640]{1,0:T(8,128)(2,1)S(1)} collective-permute-done((bf16[32,640]{1,0:T(8,128)(2,1)S(1)}, bf16[32,640]{1,0:T(8,128)(2,1)S(1)}, u32[]{:S(2)}, u32[]{:S(2)}) %collective-permute-start.7) | collective-permute-done | bytes 40992 | tf_op jit(solution)/shard_map/ppermute | solution.py:145
  28.5 1.0 %collective-permute-done.6.refs_2_ = bf16[32,640]{1,0:T(8,128)(2,1)S(1)} collective-permute-done((bf16[32,640]{1,0:T(8,128)(2,1)S(1)}, bf16[32,640]{1,0:T(8,128)(2,1)S(1)}, u32[]{:S(2)}, u32[]{:S(2)}) %collective-permute-start.6) | collective-permute-done | bytes 40992 | tf_op jit(solution)/shard_map/ppermute | solution.py:145
  29.6 0.9 %collective-permute-done.5.refs_1_ = bf16[32,640]{1,0:T(8,128)(2,1)S(1)} collective-permute-done((bf16[32,640]{1,0:T(8,128)(2,1)S(1)}, bf16[32,640]{1,0:T(8,128)(2,1)S(1)}, u32[]{:S(2)}, u32[]{:S(2)}) %collective-permute-start.5) | collective-permute-done | bytes 40992 | tf_op jit(solution)/shard_map/ppermute | solution.py:145
  30.5 0.7 %place_self.1 = bf16[1,32,2560]{2,1,0:T(8,128)(2,1)} custom-call(bf16[32,640]{1,0:T(8,128)(2,1)S(1)} %mix.4.refs_0_, bf16[32,640]{1,0:T(8,128)(2,1)S(1)} %collective-permute-done.5.refs_1_, bf16[32,640]{1,0:T(8,128)(2,1)S(1)} %collective-permute-done.6.refs_2_, bf16[32,640]{1,0:T(8,128)(2,1)S(1)} %collective-permute-done.7.refs_3_), custom_call_target="tpu_custom_call" | custom-call | tf_op jit(solution)/shard_map/place_self/pallas_call | solution.py:83
  (1 shorter events, 0.0 us)
Async XLA Ops:
  2.2 20.3 %collective-permute-start.1 = (bf16[224,640]{1,0:T(8,128)(2,1)S(1)}, bf16[224,640]{1,0:T(8,128)(2,1)S(1)}, u32[]{:S(2)}, u32[]{:S(2)}) collective-permute-start(bf16[224,640]{1,0:T(8,128)(2,1)S(1)} %get-tuple-element.27), channel_id=1, source_target_pairs={{0,4},{2,6},{4,0},{6,2},{8,12},{10,14},{12,8},{14,10},{1,5},{3,7},... | collective-permute-start | bytes 860168 | tf_op jit(solution)/shard_map/ppermute | solution.py:145
  5.2 13.7 %collective-permute-start.4 = (bf16[128,640]{1,0:T(8,128)(2,1)S(1)}, bf16[128,640]{1,0:T(8,128)(2,1)S(1)}, u32[]{:S(2)}, u32[]{:S(2)}) collective-permute-start(bf16[128,640]{1,0:T(8,128)(2,1)S(1)} %get-tuple-element.30), channel_id=1, source_target_pairs={{0,12},{2,14},{4,8},{6,10},{8,4},{10,6},{12,0},{14,2},{1,13},{3,15... | collective-permute-start | bytes 491528 | tf_op jit(solution)/shard_map/ppermute | solution.py:145
  7.7 14.5 %collective-permute-start.3 = (bf16[128,640]{1,0:T(8,128)(2,1)S(1)}, bf16[128,640]{1,0:T(8,128)(2,1)S(1)}, u32[]{:S(2)}, u32[]{:S(2)}) collective-permute-start(bf16[128,640]{1,0:T(8,128)(2,1)S(1)} %get-tuple-element.29.refs_4_.refs_6_), channel_id=1, source_target_pairs={{0,8},{2,10},{4,12},{6,14},{8,0},{10,2},{12,4},{14,6},{1,9},{3,11}... | collective-permute-start | bytes 491528 | tf_op jit(solution)/shard_map/ppermute | solution.py:145
  7.8 5.2 %collective-permute-start.8 = (bf16[32,1280]{1,0:T(8,128)(2,1)S(1)}, bf16[32,1280]{1,0:T(8,128)(2,1)S(1)}, u32[]{:S(2)}, u32[]{:S(2)}) collective-permute-start(bf16[32,1280]{1,0:T(8,128)(2,1)S(1)} %get-tuple-element.42), channel_id=1, source_target_pairs={{0,2},{2,0},{4,6},{6,4},{8,10},{10,8},{12,14},{14,12},{1,3},{3,1},... | collective-permute-start | bytes 245768 | tf_op jit(solution)/shard_map/ppermute | solution.py:145
  9.3 7.6 %collective-permute-start = (bf16[96,640]{1,0:T(8,128)(2,1)S(1)}, bf16[96,640]{1,0:T(8,128)(2,1)S(1)}, u32[]{:S(2)}, u32[]{:S(2)}) collective-permute-start(bf16[96,640]{1,0:T(8,128)(2,1)S(1)} %get-tuple-element.26), channel_id=1, source_target_pairs={{0,2},{2,0},{4,6},{6,4},{8,10},{10,8},{12,14},{14,12},{1,3},{3,1},... | collective-permute-start | bytes 368648 | tf_op jit(solution)/shard_map/ppermute | solution.py:145
  13.1 9.4 %collective-permute-start.2 = (bf16[96,640]{1,0:T(8,128)(2,1)S(1)}, bf16[96,640]{1,0:T(8,128)(2,1)S(1)}, u32[]{:S(2)}, u32[]{:S(2)}) collective-permute-start(bf16[96,640]{1,0:T(8,128)(2,1)S(1)} %get-tuple-element.28), channel_id=1, source_target_pairs={{0,6},{2,4},{4,2},{6,0},{8,14},{10,12},{12,10},{14,8},{1,7},{3,5},... | collective-permute-start | bytes 368648 | tf_op jit(solution)/shard_map/ppermute | solution.py:145
  17.8 9.5 %collective-permute-start.9 = (bf16[32,1280]{1,0:T(8,128)(2,1)S(1)}, bf16[32,1280]{1,0:T(8,128)(2,1)S(1)}, u32[]{:S(2)}, u32[]{:S(2)}) collective-permute-start(bf16[32,1280]{1,0:T(8,128)(2,1)S(1)} %get-tuple-element.47), channel_id=1, source_target_pairs={{0,2},{2,0},{4,6},{6,4},{8,10},{10,8},{12,14},{14,12},{1,3},{3,1},... | collective-permute-start | bytes 245768 | tf_op jit(solution)/shard_map/ppermute | solution.py:145
  23.2 5.3 %collective-permute-start.7 = (bf16[32,640]{1,0:T(8,128)(2,1)S(1)}, bf16[32,640]{1,0:T(8,128)(2,1)S(1)}, u32[]{:S(2)}, u32[]{:S(2)}) collective-permute-start(bf16[32,640]{1,0:T(8,128)(2,1)S(1)} %mix.7), channel_id=1, source_target_pairs={{0,6},{2,4},{4,2},{6,0},{8,14},{10,12},{12,10},{14,8},{1,7},{3,5},... | collective-permute-start | bytes 122888 | tf_op jit(solution)/shard_map/ppermute | solution.py:145
  25.5 4.1 %collective-permute-start.6 = (bf16[32,640]{1,0:T(8,128)(2,1)S(1)}, bf16[32,640]{1,0:T(8,128)(2,1)S(1)}, u32[]{:S(2)}, u32[]{:S(2)}) collective-permute-start(bf16[32,640]{1,0:T(8,128)(2,1)S(1)} %mix.6), channel_id=1, source_target_pairs={{0,4},{2,6},{4,0},{6,2},{8,12},{10,14},{12,8},{14,10},{1,5},{3,7},... | collective-permute-start | bytes 122888 | tf_op jit(solution)/shard_map/ppermute | solution.py:145
  26.4 4.1 %collective-permute-start.5 = (bf16[32,640]{1,0:T(8,128)(2,1)S(1)}, bf16[32,640]{1,0:T(8,128)(2,1)S(1)}, u32[]{:S(2)}, u32[]{:S(2)}) collective-permute-start(bf16[32,640]{1,0:T(8,128)(2,1)S(1)} %mix.5), channel_id=1, source_target_pairs={{0,2},{2,0},{4,6},{6,4},{8,10},{10,8},{12,14},{14,12},{1,3},{3,1},... | collective-permute-start | bytes 122888 | tf_op jit(solution)/shard_map/ppermute | solution.py:145
where the time goes:
time: 31.4 us; the launch traced here: 31.2 us
  starting transfers between devices  14.5 us (46%)
  waiting for transfers between devices  9.23 us (29%)
  Pallas kernels  6.71 us (21%)
  between operations  0.71 us (2%)
    ppermute x10, starting transfers between devices, moved(): return lax.ppermute(array, axes, pairs)  14.5 us
    ppermute x10, waiting for transfers between devices, moved(): return lax.ppermute(array, axes, pairs)  9.23 us
    pallas_call x11, Pallas kernels, call(): pl.pallas_call(kernel, out_shape=out_shape, in_specs=[in_spec] * len(oper...  6.71 us
  transfers between devices with their start and end apart: 10, of which 7 were waited for; matrix products, arithmetic and copies ran while one was open for 0% of the time, Pallas kernels for 14%

commit v1 on v0

--- a/solution.py
+++ b/solution.py
@@ -9,6 +9,7 @@
 
 HD = 128
 SCALE = 1.0 / math.sqrt(HD)
+TERMS = 3
 
 
 def scores_of(queries, keys):
@@ -24,10 +25,30 @@
 
 
 def softmax_parts(scores):
-    weights = jnp.exp(scores - jnp.max(scores, axis=-1, keepdims=True))
+    tops = jnp.max(scores, axis=-1, keepdims=True)
+    weights = jnp.exp(scores - tops)
     totals = jnp.sum(weights, axis=-1, keepdims=True)
-    shares = jnp.broadcast_to(1.0 / totals, (scores.shape[0], HD))
-    return weights.astype(jnp.bfloat16), shares
+    shape = (scores.shape[0], HD)
+    shares = jnp.broadcast_to(1.0 / totals, shape)
+    logs = jnp.broadcast_to(tops + jnp.log(totals), shape)
+    return weights.astype(jnp.bfloat16), shares, logs
+
+
+def lanes_of_logs(logs):
+    lane = lax.broadcasted_iota(jnp.int32, logs[0].shape, 1)
+    block = jnp.zeros(logs[0].shape, jnp.float32)
+    for head, rest in enumerate(logs):
+        for term in range(TERMS):
+            part = rest.astype(jnp.bfloat16).astype(jnp.float32)
+            block = jnp.where(lane == TERMS * head + term, part, block)
+            rest = rest - part
+    return block.astype(jnp.bfloat16)
+
+
+def logs_of_lanes(block, head):
+    lane = lax.broadcasted_iota(jnp.int32, (HD, HD), 0)
+    picked = (lane >= TERMS * head) & (lane < TERMS * (head + 1))
+    return weighted(block, jnp.where(picked, 1.0, 0.0).astype(block.dtype))
 
 
 def run_all(copies, sems):
@@ -62,7 +83,9 @@
         scores = scores_of(
             jnp.concatenate([ref[:, lanes] for ref in queries], axis=0), key_ref[0, :, lanes]
         )
-        weights_ref[head], shares_ref[head] = softmax_parts(jnp.where(usable, scores, -jnp.inf))
+        weights_ref[head], shares_ref[head], _ = softmax_parts(
+            jnp.where(usable, scores, -jnp.inf)
+        )
     for head in range(cols // HD):
         lanes = head_lanes(head)
         mixed = weighted(weights_ref[head], value_ref[0, :, lanes]) * shares_ref[head]
@@ -150,17 +173,21 @@
             start = pl.multiple_of(shard * cols + member * width, HD)
             return ref.at[0, :, pl.ds(start, size)]
 
+        over_patch = [mate for mate in mates if mate[0] != 0]
+        near_blocks = [(turn, shift) for turn in range(shards) for shift in range(1, share)]
+        near_width = len(near_blocks) * width
         stale_rows = 2 * patch_rows
 
         def fresh_start(shift, turn):
             return stale_rows if turn == 0 and shift != 0 else 0
 
         def message_rows(shift, turn):
-            return fresh_start(shift, turn) + 3 * rows
+            return fresh_start(shift, turn) + (3 if shift == 0 else 1) * rows
 
         def pack_kernel(query, key, value, old_key, old_value, cross, *refs):
             stale, own, refs = refs[:share], refs[share], refs[share + 1 :]
-            crosses, messages = refs[:shards], refs[shards:-1]
+            crosses, messages = refs[:shards], refs[shards : shards + len(mates)]
+            nears = refs[shards + len(mates) : -1]
             me = lax.rem(lax.axis_index("patch"), share)
             copies = []
 
@@ -172,7 +199,7 @@
                     copies.append((source.at[0, :, lanes], target.at[block]))
 
             def fresh_copies(shift, turn, target, first):
-                for index, source in enumerate((query, key, value)):
+                for index, source in enumerate((query, key, value)[: 3 if shift == 0 else 1]):
                     block = pl.ds(first + index * rows, rows)
                     copies.append((place_of(shift, turn, source, width), target.at[block]))
 
@@ -188,6 +215,11 @@
                 shard = lax.rem(lax.axis_index("head") + turn, shards)
                 lanes = pl.ds(pl.multiple_of(shard * cols, HD), cols)
                 copies.append((cross.at[0, :, lanes], target))
+            for turn, target in enumerate(nears):
+                for index, source in enumerate((query, key, value)[0 if turn == 0 else 1 :]):
+                    for place, (other, shift) in enumerate(near_blocks):
+                        block = target.at[pl.ds(index * rows, rows), pl.ds(place * width, width)]
+                        copies.append((place_of(shift, turn + other, source, width), block))
             run_all(copies, refs[-1])
 
         packed_shapes = (
@@ -196,9 +228,12 @@
             + [(rows, cols)] * shards
             + [(message_rows(*mate), width) for mate in mates]
         )
+        if near_blocks:
+            packed_shapes += [(3 * rows, near_width)] + [(2 * rows, near_width)] * (shards - 1)
         copy_count = 2 * share + 3 + shards + sum(
-            3 + (2 if fresh_start(*mate) else 0) for mate in mates
-        )
+            (3 if mate[0] == 0 else 1) + (2 if fresh_start(*mate) else 0) for mate in mates
+        )
+        copy_count += len(near_blocks) * (2 * shards + 1)
         packed = call(
             pack_kernel,
             "pack",
@@ -208,7 +243,9 @@
             scratch=[pltpu.SemaphoreType.DMA((copy_count,))],
         )
         stale, own, packed = packed[:share], packed[share], packed[share + 1 :]
-        crosses, messages = packed[:shards], packed[shards:]
+        crosses, messages = packed[:shards], packed[shards : shards + len(mates)]
+        nears = packed[shards + len(mates) :]
+        nears = [a if turn == 0 else moved(a, 0, 0, turn) for turn, a in enumerate(nears)]
         arrived = [
             moved(message, 0, *mate) for mate, message in zip(mates, messages)
         ]
@@ -274,6 +311,28 @@
             scratch=[pltpu.SemaphoreType.DMA((shards,))],
         )
 
+        def near_kernel(*refs):
+            own_ref, others, (sums_ref, logs_ref) = refs[0], refs[1:-2], refs[-2:]
+            for index in range(near_width // HD):
+                lanes = head_lanes(index)
+                keys = [own_ref[rows : 2 * rows, lanes]] + [ref[:rows, lanes] for ref in others]
+                values = [own_ref[2 * rows :, lanes]] + [ref[rows:, lanes] for ref in others]
+                scores = scores_of(own_ref[:rows, lanes], jnp.concatenate(keys, axis=0))
+                weights, shares, logs_ref[index] = softmax_parts(scores)
+                sums_ref[:, lanes] = weighted(weights, jnp.concatenate(values, axis=0)) * shares
+
+        near = []
+        if near_blocks:
+            near = call(
+                near_kernel,
+                "near",
+                [
+                    pltpu.VMEM((rows, near_width), jnp.float32),
+                    pltpu.VMEM((near_width // HD, rows, HD), jnp.float32),
+                ],
+                nears,
+            )
+
         spots = [(0, 0)] + mates
         tokens = [own, *arrived]
         first_row = dict(zip(spots, [0] + [fresh_start(*mate) for mate in mates]))
@@ -298,13 +357,16 @@
             return [ref[block, lanes] for ref in found + others]
 
         def weights_kernel(*refs):
-            sources, targets = refs[: -2 * len(spots)], refs[-2 * len(spots) :]
+            count = len(spots) + 1 + len(pieces)
+            sources, targets, logs_of = refs[:count], refs[count:], {}
             for head in range(share_heads):
                 lanes = head_lanes(head)
                 for shift in range(share):
                     queries = token_rows(sources, shift, 0, lanes)
-                    keys = token_rows(sources, shift, 1, lanes) + stale_of(sources, shift, 0, lanes)
-                    weights, shares = softmax_parts(
+                    keys = stale_of(sources, shift, 0, lanes)
+                    if shift == 0:
+                        keys = token_rows(sources, shift, 1, lanes) + keys
+                    weights, shares, logs = softmax_parts(
                         scores_of(jnp.concatenate(queries, axis=0), jnp.concatenate(keys, axis=0))
                     )
                     for turn in range(shards):
@@ -312,33 +374,61 @@
                         block = slice(turn * rows, (turn + 1) * rows)
                         targets[2 * spot][head] = weights[block]
                         targets[2 * spot + 1][head] = shares[block]
+                        logs_of.setdefault(spot, []).append(logs[block])
+            for place, mate in enumerate(over_patch):
+                targets[2 * len(spots) + place][...] = lanes_of_logs(logs_of[spots.index(mate)])
 
         def mix_kernel(shift, weights_ref, shares_ref, *refs):
             sources, target = refs[:-1], refs[-1]
             for head in range(share_heads):
                 lanes = head_lanes(head)
-                values = token_rows(sources, shift, 2, lanes) + stale_of(sources, shift, 1, lanes)
+                values = stale_of(sources, shift, 1, lanes)
+                if shift == 0:
+                    values = token_rows(sources, shift, 2, lanes) + values
                 mixed = weighted(weights_ref[head], jnp.concatenate(values, axis=0))
                 target[:, lanes] = (mixed * shares_ref[head]).astype(target.dtype)
 
+        def mate_mix_kernel(shift, weights_ref, shares_ref, logs_ref, *refs):
+            mix_kernel(shift, weights_ref, shares_ref, *refs[:-1], refs[-1].at[:, pl.ds(0, width)])
+            refs[-1][:, width:] = logs_ref[...]
+
+        def merge_kernel(*refs):
+            (sums_ref, logs_ref), refs = refs[:2], refs[2:]
+            for (shift, turn), far, target in zip(over_patch, refs, refs[len(over_patch) :]):
+                first = near_blocks.index((turn, shift)) * share_heads
+                for head in range(share_heads):
+                    lanes = head_lanes(head)
+                    far_logs, near_logs = logs_of_lanes(far[:, width:], head), logs_ref[first + head]
+                    tops = jnp.maximum(far_logs, near_logs)
+                    far_part, near_part = jnp.exp(far_logs - tops), jnp.exp(near_logs - tops)
+                    mixed = far[:, lanes].astype(jnp.float32) * far_part
+                    mixed += sums_ref[:, head_lanes(first + head)] * near_part
+                    target[:, lanes] = (mixed / (far_part + near_part)).astype(target.dtype)
+
         sources = (*tokens, stale[0], *pieces)
+        part_shapes = []
+        for shift, _ in spots:
+            seen = patch_rows * (patches if shift == 0 else patches - 1)
+            part_shapes += [
+                pltpu.VMEM((share_heads, rows, seen), kind),
+                pltpu.VMEM((share_heads, rows, HD), jnp.float32),
+            ]
         parts = call(
             weights_kernel,
             "weights",
-            [
-                pltpu.VMEM((share_heads, rows, patch_rows * patches), kind),
-                pltpu.VMEM((share_heads, rows, HD), jnp.float32),
-            ]
-            * len(spots),
+            part_shapes + [pltpu.VMEM((rows, HD), kind)] * len(over_patch),
             sources,
         )
 
         def mixed(spot):
+            pair, shift = parts[2 * spot : 2 * spot + 2], spots[spot][0]
+            if shift == 0:
+                kernel, shape = mix_kernel, (rows, width)
+            else:
+                kernel, shape = mate_mix_kernel, (rows, width + HD)
+                pair = (*pair, parts[2 * len(spots) + over_patch.index(spots[spot])])
             return call(
-                lambda *refs: mix_kernel(spots[spot][0], *refs),
-                "mix",
-                pltpu.VMEM((rows, width), kind),
-                (*parts[2 * spot : 2 * spot + 2], *sources),
+                lambda *refs: kernel(shift, *refs), "mix", pltpu.VMEM(shape, kind), (*pair, *sources)
             )
 
         back = [
@@ -346,6 +436,13 @@
             for index, (shift, turn) in enumerate(spots)
             if index > 0
         ]
+        if over_patch:
+            back[shards - 1 :] = call(
+                merge_kernel,
+                "merge",
+                [pltpu.VMEM((rows, width), kind)] * len(over_patch),
+                (*near, *back[shards - 1 :]),
+            )
         self_mixed = call(
             lambda *refs: place_kernel(spots, width, *refs),
             "place_self",

time: 31.4 us -> 31.8 us (1.013)
  waiting for transfers between devices: 9.23 us -> 5.83 us
  Pallas kernels: 6.71 us -> 9.38 us
  starting transfers between devices: 14.5 us -> 15.6 us
    ppermute x10 -> x11, waiting for transfers between devices: 9.23 us -> 5.83 us  [moved(): return lax.ppermute(array, axes, pairs)]
    pallas_call x11 -> x13, Pallas kernels: 6.71 us -> 9.38 us  [call(): pl.pallas_call(kernel, out_shape=out_shape, in_specs=[in_spec] * len(oper...]
    ppermute x10 -> x11, starting transfers between devices: 14.5 us -> 15.6 us  [moved(): return lax.ppermute(array, axes, pairs)]
  transfers between devices with their start and end apart: 10 -> 11, of which waited for: 7 -> 3; matrix products, arithmetic and copies ran while one was open for 0% -> 0% of each run, Pallas kernels for 14% -> 23%
where the time goes in v1:
time: 31.8 us; the launch traced here: 31.6 us
  starting transfers between devices  15.6 us (49%)
  Pallas kernels  9.38 us (29%)
  waiting for transfers between devices  5.83 us (18%)
  between operations  0.74 us (2%)
    ppermute x11, starting transfers between devices, moved(): return lax.ppermute(array, axes, pairs)  15.6 us
    pallas_call x13, Pallas kernels, call(): pl.pallas_call(kernel, out_shape=out_shape, in_specs=[in_spec] * len(oper...  9.38 us
    ppermute x11, waiting for transfers between devices, moved(): return lax.ppermute(array, axes, pairs)  5.83 us
  transfers between devices with their start and end apart: 11, of which 3 were waited for; matrix products, arithmetic and copies ran while one was open for 0% of the time, Pallas kernels for 23%

profile of v1, /device:TPU:0, one launch (start us, length us, event | category | flops | bytes accessed | tf_op | source)
XLA Modules:
  0.0 31.6 jit_solution(12007945422527304206)
XLA Ops:
  0.6 1.6 %pack.1 = (bf16[128,640]{1,0:T(8,128)(2,1)S(1)}, bf16[128,640]{1,0:T(8,128)(2,1)S(1)}, bf16[96,640]{1,0:T(8,128)(2,1)S(1)}, bf16[32,1280]{1,0:T(8,128)(2,1)S(1)}...) custom-call(bf16[1,32,2560]{2,1,0:T(8,128)(2,1)} %query.1, ...), custom_call_target="tpu_custom_call" | custom-call | tf_op jit(solution)/shard_map/pack/pallas_call | solution.py:106
  2.2 5.1 %collective-permute-start.4 = (bf16[128,640]{1,0:T(8,128)(2,1)S(1)}, bf16[128,640]{1,0:T(8,128)(2,1)S(1)}, u32[]{:S(2)}, u32[]{:S(2)}) collective-permute-start(bf16[128,640]{1,0:T(8,128)(2,1)S(1)} %get-tuple-element.38), channel_id=1, source_target_pairs={{0,12},{2,14},{4,8},{6,10},{8,4},{10,6},{12,0},{14,2},{1,13},{3,15... | collective-permute-start | bytes 491528 | tf_op jit(solution)/shard_map/ppermute | solution.py:168
  7.3 0.0 collective-permute-start.3
  7.3 0.6 %collective-permute-start.1 = (bf16[160,640]{1,0:T(8,128)(2,1)S(1)}, bf16[160,640]{1,0:T(8,128)(2,1)S(1)}, u32[]{:S(2)}, u32[]{:S(2)}) collective-permute-start(bf16[160,640]{1,0:T(8,128)(2,1)S(1)} %get-tuple-element.35), channel_id=1, source_target_pairs={{0,4},{2,6},{4,0},{6,2},{8,12},{10,14},{12,8},{14,10},{1,5},{3,7},... | collective-permute-start | bytes 614408 | tf_op jit(solution)/shard_map/ppermute | solution.py:168
  7.9 1.6 %collective-permute-start.9 = (bf16[32,1280]{1,0:T(8,128)(2,1)S(1)}, bf16[32,1280]{1,0:T(8,128)(2,1)S(1)}, u32[]{:S(2)}, u32[]{:S(2)}) collective-permute-start(bf16[32,1280]{1,0:T(8,128)(2,1)S(1)} %get-tuple-element.58), channel_id=1, source_target_pairs={{0,2},{2,0},{4,6},{6,4},{8,10},{10,8},{12,14},{14,12},{1,3},{3,1},... | collective-permute-start | bytes 245768 | tf_op jit(solution)/shard_map/ppermute | solution.py:168
  9.6 0.4 %collective-permute-start = (bf16[96,640]{1,0:T(8,128)(2,1)S(1)}, bf16[96,640]{1,0:T(8,128)(2,1)S(1)}, u32[]{:S(2)}, u32[]{:S(2)}) collective-permute-start(bf16[96,640]{1,0:T(8,128)(2,1)S(1)} %get-tuple-element.34), channel_id=1, source_target_pairs={{0,2},{2,0},{4,6},{6,4},{8,10},{10,8},{12,14},{14,12},{1,3},{3,1},... | collective-permute-start | bytes 368648 | tf_op jit(solution)/shard_map/ppermute | solution.py:168
  10.0 3.2 %collective-permute-done.9.refs_1_ = bf16[32,1280]{1,0:T(8,128)(2,1)S(1)} collective-permute-done((bf16[32,1280]{1,0:T(8,128)(2,1)S(1)}, bf16[32,1280]{1,0:T(8,128)(2,1)S(1)}, u32[]{:S(2)}, u32[]{:S(2)}) %collective-permute-start.9) | collective-permute-done | bytes 81952 | tf_op jit(solution)/shard_map/ppermute | solution.py:168
  13.2 1.2 %collective-permute-start.6 = (bf16[64,1280]{1,0:T(8,128)(2,1)S(1)}, bf16[64,1280]{1,0:T(8,128)(2,1)S(1)}, u32[]{:S(2)}, u32[]{:S(2)}) collective-permute-start(bf16[64,1280]{1,0:T(8,128)(2,1)S(1)} %get-tuple-element.46), channel_id=1, source_target_pairs={{0,2},{2,0},{4,6},{6,4},{8,10},{10,8},{12,14},{14,12},{1,3},{3,1},... | collective-permute-start | bytes 491528 | tf_op jit(solution)/shard_map/ppermute | solution.py:168
  14.4 1.7 %load.1 = (bf16[1,512,1280]{2,1,0:T(8,128)(2,1)S(1)}, bf16[1,512,1280]{2,1,0:T(8,128)(2,1)S(1)}, s32[1,512]{1,0:T(1,128)S(1)}) custom-call(bf16[1,512,1280]{2,1,0:T(8,128)(2,1)} %refs_0_.1, bf16[1,512,1280]{2,1,0:T(8,128)(2,1)} %refs_1_.1, s32[1,512]{1,0:T(1,128)} %refs_2_.1), custom_call_target="tpu_custom_call" | custom-call | tf_op jit(solution)/shard_map/load/pallas_call | solution.py:106
  16.1 0.0 collective-permute-done.refs_1_.refs_3_.refs_4_.refs_5_
  16.1 1.7 %collective-permute-start.2 = (bf16[32,640]{1,0:T(8,128)(2,1)S(1)}, bf16[32,640]{1,0:T(8,128)(2,1)S(1)}, u32[]{:S(2)}, u32[]{:S(2)}) collective-permute-start(bf16[32,640]{1,0:T(8,128)(2,1)S(1)} %get-tuple-element.36), channel_id=1, source_target_pairs={{0,6},{2,4},{4,2},{6,0},{8,14},{10,12},{12,10},{14,8},{1,7},{3,5},... | collective-permute-start | bytes 122888 | tf_op jit(solution)/shard_map/ppermute | solution.py:168
  17.9 0.9 %cross.3 = (bf16[32,1280]{1,0:T(8,128)(2,1)S(1)}, bf16[32,1280]{1,0:T(8,128)(2,1)S(1)}) custom-call(bf16[32,1280]{1,0:T(8,128)(2,1)S(1)} %get-tuple-element.57.refs_0_, bf16[32,1280]{1,0:T(8,128)(2,1)S(1)} %collective-permute-done.9.refs_1_, bf16[1,512,1280]{2,1,0:T(8,128)(2,1)S(1)} %get-tuple-element.59.refs_2_, ...), custom_call_target="tpu_custom_call" | custom-call | tf_op jit(solution)/shard_map/cross/pallas_call | solution.py:106
  18.7 0.0 collective-permute-done.4.refs_1_
  18.7 1.2 %collective-permute-start.10 = (bf16[32,1280]{1,0:T(8,128)(2,1)S(1)}, bf16[32,1280]{1,0:T(8,128)(2,1)S(1)}, u32[]{:S(2)}, u32[]{:S(2)}) collective-permute-start(bf16[32,1280]{1,0:T(8,128)(2,1)S(1)} %get-tuple-element.63), channel_id=1, source_target_pairs={{0,2},{2,0},{4,6},{6,4},{8,10},{10,8},{12,14},{14,12},{1,3},{3,1},... | collective-permute-start | bytes 245768 | tf_op jit(solution)/shard_map/ppermute | solution.py:168
  20.0 1.3 %collective-permute-done.3.refs_0_ = bf16[128,640]{1,0:T(8,128)(2,1)S(1)} collective-permute-done((bf16[128,640]{1,0:T(8,128)(2,1)S(1)}, bf16[128,640]{1,0:T(8,128)(2,1)S(1)}, u32[]{:S(2)}, u32[]{:S(2)}) %collective-permute-start.3) | collective-permute-done | bytes 163872 | tf_op jit(solution)/shard_map/ppermute | solution.py:168
  21.3 1.3 %collective-permute-done.2.refs_3_.refs_5_.refs_6_ = bf16[32,640]{1,0:T(8,128)(2,1)S(1)} collective-permute-done((bf16[32,640]{1,0:T(8,128)(2,1)S(1)}, bf16[32,640]{1,0:T(8,128)(2,1)S(1)}, u32[]{:S(2)}, u32[]{:S(2)}) %collective-permute-start.2) | collective-permute-done | bytes 40992 | tf_op jit(solution)/shard_map/ppermute | solution.py:168
  22.6 0.0 collective-permute-done.1.refs_2_.refs_4_.refs_5_
  22.6 0.6 %weights.1 = (bf16[5,32,256]{2,1,0:T(8,128)(2,1)S(1)}, f32[5,32,128]{2,1,0:T(8,128)S(1)}, bf16[5,32,256]{2,1,0:T(8,128)(2,1)S(1)}, f32[5,32,128]{2,1,0:T(8,128)S...) custom-call(bf16[96,640]{1,0:T(8,128)(2,1)S(1)} %get-tuple-element.3, ...), custom_call_target="tpu_custom_call" | custom-call | tf_op jit(solution)/shard_map/weights/pallas_call | solution.py:106
  23.2 0.2 mix.7
  23.3 0.5 %collective-permute-start.8 = (bf16[32,768]{1,0:T(8,128)(2,1)S(1)}, bf16[32,768]{1,0:T(8,128)(2,1)S(1)}, u32[]{:S(2)}, u32[]{:S(2)}) collective-permute-start(bf16[32,768]{1,0:T(8,128)(2,1)S(1)} %mix.7), channel_id=1, source_target_pairs={{0,6},{2,4},{4,2},{6,0},{8,14},{10,12},{12,10},{14,8},{1,7},{3,5},... | collective-permute-start | bytes 147464 | tf_op jit(solution)/shard_map/ppermute | solution.py:168
  23.8 0.2 mix.6
  24.0 1.6 %collective-permute-start.7 = (bf16[32,768]{1,0:T(8,128)(2,1)S(1)}, bf16[32,768]{1,0:T(8,128)(2,1)S(1)}, u32[]{:S(2)}, u32[]{:S(2)}) collective-permute-start(bf16[32,768]{1,0:T(8,128)(2,1)S(1)} %mix.6), channel_id=1, source_target_pairs={{0,4},{2,6},{4,0},{6,2},{8,12},{10,14},{12,8},{14,10},{1,5},{3,7},... | collective-permute-start | bytes 147464 | tf_op jit(solution)/shard_map/ppermute | solution.py:168
  25.6 0.2 mix.5
  25.8 1.6 %collective-permute-start.5 = (bf16[32,640]{1,0:T(8,128)(2,1)S(1)}, bf16[32,640]{1,0:T(8,128)(2,1)S(1)}, u32[]{:S(2)}, u32[]{:S(2)}) collective-permute-start(bf16[32,640]{1,0:T(8,128)(2,1)S(1)} %mix.5), channel_id=1, source_target_pairs={{0,2},{2,0},{4,6},{6,4},{8,10},{10,8},{12,14},{14,12},{1,3},{3,1},... | collective-permute-start | bytes 122888 | tf_op jit(solution)/shard_map/ppermute | solution.py:168
  27.4 0.0 collective-permute-done.6.refs_1_
  27.4 2.3 %near.1 = (f32[32,1280]{1,0:T(8,128)S(1)}, f32[10,32,128]{2,1,0:T(8,128)S(1)}) custom-call(bf16[96,1280]{1,0:T(8,128)(2,1)S(1)} %get-tuple-element.45.refs_0_, bf16[64,1280]{1,0:T(8,128)(2,1)S(1)} %collective-permute-done.6.refs_1_), custom_call_target="tpu_custom_call" | custom-call | tf_op jit(solution)/shard_map/near/pallas_call | solution.py:106
  29.7 0.2 mix.4.refs_0_
  29.9 0.0 collective-permute-done.10.refs_1_
  29.9 0.7 %place_cross.1 = bf16[1,32,2560]{2,1,0:T(8,128)(2,1)} custom-call(bf16[32,1280]{1,0:T(8,128)(2,1)S(1)} %get-tuple-element.62.refs_0_, bf16[32,1280]{1,0:T(8,128)(2,1)S(1)} %collective-permute-done.10.refs_1_), custom_call_target="tpu_custom_call" | custom-call | tf_op jit(solution)/shard_map/place_cross/pallas_call | solution.py:106
  30.6 0.0 collective-permute-done.8.refs_3_
  30.6 0.0 collective-permute-done.7.refs_2_
  30.6 0.2 merge.1
  30.8 0.0 collective-permute-done.5.refs_1_
  30.9 0.7 %place_self.1 = bf16[1,32,2560]{2,1,0:T(8,128)(2,1)} custom-call(bf16[32,640]{1,0:T(8,128)(2,1)S(1)} %mix.4.refs_0_, bf16[32,640]{1,0:T(8,128)(2,1)S(1)} %collective-permute-done.5.refs_1_, bf16[32,640]{1,0:T(8,128)(2,1)S(1)} %get-tuple-element.55.refs_2_, bf16[32,640]{1,0:T(8,128)(2,1)S(1)} %get-tuple-element.56.refs_3_), custom_call_target="tpu_custom_call" | custom-call | tf_op jit(solution)/shard_map/place_self/pallas_call | solution.py:106
  (1 shorter events, 0.0 us)
Async XLA Ops:
  2.2 16.5 %collective-permute-start.4 = (bf16[128,640]{1,0:T(8,128)(2,1)S(1)}, bf16[128,640]{1,0:T(8,128)(2,1)S(1)}, u32[]{:S(2)}, u32[]{:S(2)}) collective-permute-start(bf16[128,640]{1,0:T(8,128)(2,1)S(1)} %get-tuple-element.38), channel_id=1, source_target_pairs={{0,12},{2,14},{4,8},{6,10},{8,4},{10,6},{12,0},{14,2},{1,13},{3,15... | collective-permute-start | bytes 491528 | tf_op jit(solution)/shard_map/ppermute | solution.py:168
  7.3 14.0 %collective-permute-start.3 = (bf16[128,640]{1,0:T(8,128)(2,1)S(1)}, bf16[128,640]{1,0:T(8,128)(2,1)S(1)}, u32[]{:S(2)}, u32[]{:S(2)}) collective-permute-start(bf16[128,640]{1,0:T(8,128)(2,1)S(1)} %get-tuple-element.37.refs_4_.refs_6_.refs_7_), channel_id=1, source_target_pairs={{0,8},{2,10},{4,12},{6,14},{8,0},{10,2},{12,4},{14,6},{1,9},{3,11}... | collective-permute-start | bytes 491528 | tf_op jit(solution)/shard_map/ppermute | solution.py:168
  7.3 15.3 %collective-permute-start.1 = (bf16[160,640]{1,0:T(8,128)(2,1)S(1)}, bf16[160,640]{1,0:T(8,128)(2,1)S(1)}, u32[]{:S(2)}, u32[]{:S(2)}) collective-permute-start(bf16[160,640]{1,0:T(8,128)(2,1)S(1)} %get-tuple-element.35), channel_id=1, source_target_pairs={{0,4},{2,6},{4,0},{6,2},{8,12},{10,14},{12,8},{14,10},{1,5},{3,7},... | collective-permute-start | bytes 614408 | tf_op jit(solution)/shard_map/ppermute | solution.py:168
  7.9 5.2 %collective-permute-start.9 = (bf16[32,1280]{1,0:T(8,128)(2,1)S(1)}, bf16[32,1280]{1,0:T(8,128)(2,1)S(1)}, u32[]{:S(2)}, u32[]{:S(2)}) collective-permute-start(bf16[32,1280]{1,0:T(8,128)(2,1)S(1)} %get-tuple-element.58), channel_id=1, source_target_pairs={{0,2},{2,0},{4,6},{6,4},{8,10},{10,8},{12,14},{14,12},{1,3},{3,1},... | collective-permute-start | bytes 245768 | tf_op jit(solution)/shard_map/ppermute | solution.py:168
  9.6 6.5 %collective-permute-start = (bf16[96,640]{1,0:T(8,128)(2,1)S(1)}, bf16[96,640]{1,0:T(8,128)(2,1)S(1)}, u32[]{:S(2)}, u32[]{:S(2)}) collective-permute-start(bf16[96,640]{1,0:T(8,128)(2,1)S(1)} %get-tuple-element.34), channel_id=1, source_target_pairs={{0,2},{2,0},{4,6},{6,4},{8,10},{10,8},{12,14},{14,12},{1,3},{3,1},... | collective-permute-start | bytes 368648 | tf_op jit(solution)/shard_map/ppermute | solution.py:168
  13.2 14.2 %collective-permute-start.6 = (bf16[64,1280]{1,0:T(8,128)(2,1)S(1)}, bf16[64,1280]{1,0:T(8,128)(2,1)S(1)}, u32[]{:S(2)}, u32[]{:S(2)}) collective-permute-start(bf16[64,1280]{1,0:T(8,128)(2,1)S(1)} %get-tuple-element.46), channel_id=1, source_target_pairs={{0,2},{2,0},{4,6},{6,4},{8,10},{10,8},{12,14},{14,12},{1,3},{3,1},... | collective-permute-start | bytes 491528 | tf_op jit(solution)/shard_map/ppermute | solution.py:168
  16.1 6.4 %collective-permute-start.2 = (bf16[32,640]{1,0:T(8,128)(2,1)S(1)}, bf16[32,640]{1,0:T(8,128)(2,1)S(1)}, u32[]{:S(2)}, u32[]{:S(2)}) collective-permute-start(bf16[32,640]{1,0:T(8,128)(2,1)S(1)} %get-tuple-element.36), channel_id=1, source_target_pairs={{0,6},{2,4},{4,2},{6,0},{8,14},{10,12},{12,10},{14,8},{1,7},{3,5},... | collective-permute-start | bytes 122888 | tf_op jit(solution)/shard_map/ppermute | solution.py:168
  18.7 11.2 %collective-permute-start.10 = (bf16[32,1280]{1,0:T(8,128)(2,1)S(1)}, bf16[32,1280]{1,0:T(8,128)(2,1)S(1)}, u32[]{:S(2)}, u32[]{:S(2)}) collective-permute-start(bf16[32,1280]{1,0:T(8,128)(2,1)S(1)} %get-tuple-element.63), channel_id=1, source_target_pairs={{0,2},{2,0},{4,6},{6,4},{8,10},{10,8},{12,14},{14,12},{1,3},{3,1},... | collective-permute-start | bytes 245768 | tf_op jit(solution)/shard_map/ppermute | solution.py:168
  23.3 7.2 %collective-permute-start.8 = (bf16[32,768]{1,0:T(8,128)(2,1)S(1)}, bf16[32,768]{1,0:T(8,128)(2,1)S(1)}, u32[]{:S(2)}, u32[]{:S(2)}) collective-permute-start(bf16[32,768]{1,0:T(8,128)(2,1)S(1)} %mix.7), channel_id=1, source_target_pairs={{0,6},{2,4},{4,2},{6,0},{8,14},{10,12},{12,10},{14,8},{1,7},{3,5},... | collective-permute-start | bytes 147464 | tf_op jit(solution)/shard_map/ppermute | solution.py:168
  24.0 6.6 %collective-permute-start.7 = (bf16[32,768]{1,0:T(8,128)(2,1)S(1)}, bf16[32,768]{1,0:T(8,128)(2,1)S(1)}, u32[]{:S(2)}, u32[]{:S(2)}) collective-permute-start(bf16[32,768]{1,0:T(8,128)(2,1)S(1)} %mix.6), channel_id=1, source_target_pairs={{0,4},{2,6},{4,0},{6,2},{8,12},{10,14},{12,8},{14,10},{1,5},{3,7},... | collective-permute-start | bytes 147464 | tf_op jit(solution)/shard_map/ppermute | solution.py:168
  25.8 5.0 %collective-permute-start.5 = (bf16[32,640]{1,0:T(8,128)(2,1)S(1)}, bf16[32,640]{1,0:T(8,128)(2,1)S(1)}, u32[]{:S(2)}, u32[]{:S(2)}) collective-permute-start(bf16[32,640]{1,0:T(8,128)(2,1)S(1)} %mix.5), channel_id=1, source_target_pairs={{0,2},{2,0},{4,6},{6,4},{8,10},{10,8},{12,14},{14,12},{1,3},{3,1},... | collective-permute-start | bytes 122888 | tf_op jit(solution)/shard_map/ppermute | solution.py:168
